TPU v7x, 32 devices: a whole 2x2x4 slice. The times are simulated.
32 devices in a mesh: site: 4 (over y, x), blk: 8 (over z, core).
Axes of the slice: x: 2, y: 2, z: 4, core: 2. Of those that a mesh axis runs over, the one named last changes fastest.
Arguments:
- corner: bfloat16 [4, 768, 768], P('site', 'blk'), may hold values from -6 to 6
- edge: bfloat16 [4, 768, 64, 768], P('site', 'blk'), may hold values from -0.02734375 to 0.02734375
- proj_left: bfloat16 [4, 768, 64, 768], P('site', 'blk'), may hold values from -0.21875 to 0.21875
- proj_right: bfloat16 [4, 768, 64, 768], P('site', 'blk'), may hold values from -0.21875 to 0.21875
- charge: int32 [4, 768], P('site'), may hold values from 0 to 15, never falling along the last dimension, each value on 1 to 96 neighbouring positions
- cot_left: float32 [4, 768, 768], P('site', 'blk'), may hold values from -2 to 2
- cot_right: float32 [4, 768, 768], P('site', 'blk'), may hold values from -2 to 2
Outputs:
- new_left: bfloat16 [4, 768, 768], P('site', 'blk')
- new_right: bfloat16 [4, 768, 768], P('site', 'blk')
- grad_left: bfloat16 [4, 768, 64, 768], P('site', 'blk')
- grad_right: bfloat16 [4, 768, 64, 768], P('site', 'blk')
Inputs may be any that keep to these rules, and one draw needn't show every extreme that they name: `charge`: sector labels never fall along the bond index; each sector holds 1 to 96 indices.
All inputs are finite; a program needn't handle non-finite values.
Results may differ from a plain program's by a relative error of at most 0.0059.
Values may be sent and summed in bfloat16 or wider, within the bound.
A program may use at most 128 MiB of HBM per device.

v0:
```python
import jax
import jax.numpy as jnp
from jax import lax
from jax.sharding import PartitionSpec as P

ITERS = 2


def shifted(block, axis, distance):
    devices = range(lax.axis_size(axis))
    route = [((i - distance) % len(devices), i) for i in devices]
    return lax.ppermute(block, axis, route)


def contract_first(left, right):
    return lax.dot_general(
        left, right, (((0,), (0,)), ((), ())), preferred_element_type=jnp.float32
    )


def contract_last(left, right):
    return lax.dot_general(
        left, right, (((1,), (1,)), ((), ())), preferred_element_type=jnp.float32
    )


def body(corner, edge, proj_left, proj_right, charge, cot_left, cot_right):
    rows = corner.shape[1]
    width = corner.shape[2]
    depth = edge.shape[2]
    first_row = lax.axis_index("blk") * rows
    labels = charge[0]
    own_labels = lax.dynamic_slice_in_dim(labels, first_row, rows, 0)
    mask = (own_labels[:, None] == labels[None, :]).astype(jnp.float32)
    here = corner[0]
    prev_corner = shifted(here, "site", 1)
    next_corner = shifted(here, "site", -1)
    edge_flat = edge[0].reshape(rows * depth, width)
    left_flat = proj_left[0].reshape(rows * depth, width)
    right_flat = proj_right[0].reshape(rows * depth, width)

    def partial_term(flat_proj):
        return contract_first(edge_flat, flat_proj)

    part_left = lax.psum_scatter(partial_term(left_flat), "blk", scatter_dimension=0, tiled=True)
    part_right = lax.psum_scatter(partial_term(right_flat), "blk", scatter_dimension=0, tiled=True)
    enl_left, enl_right = (
        lax.all_gather(part_left.astype(jnp.bfloat16), "blk", axis=0, tiled=True),
        lax.all_gather(part_right.astype(jnp.bfloat16), "blk", axis=0, tiled=True),
    )
    new_left = (mask * jnp.dot(prev_corner, enl_left, preferred_element_type=jnp.float32)).astype(
        jnp.bfloat16
    )
    new_right = (mask * jnp.dot(next_corner, enl_right, preferred_element_type=jnp.float32)).astype(
        jnp.bfloat16
    )
    adj_left = cot_left[0]
    adj_right = cot_right[0]
    for step in range(ITERS):
        w_left = (mask * adj_left).astype(jnp.bfloat16)
        w_right = (mask * adj_right).astype(jnp.bfloat16)
        back_left = contract_last(w_left, enl_left)
        back_right = contract_last(w_right, enl_right)
        adj_left = cot_left[0] + shifted(back_left, "site", -1)
        adj_right = cot_right[0] + shifted(back_right, "site", 1)
    w_left = (mask * adj_left).astype(jnp.bfloat16)
    w_right = (mask * adj_right).astype(jnp.bfloat16)
    full_prev, full_next, full_wl, full_wr = (
        lax.all_gather(prev_corner, "blk", axis=0, tiled=True),
        lax.all_gather(next_corner, "blk", axis=0, tiled=True),
        lax.all_gather(w_left, "blk", axis=0, tiled=True),
        lax.all_gather(w_right, "blk", axis=0, tiled=True),
    )
    mid_whole_left = contract_first(full_prev, full_wl).astype(jnp.bfloat16)
    mid_whole_right = contract_first(full_next, full_wr).astype(jnp.bfloat16)
    grad_flat_left = jnp.dot(edge_flat, mid_whole_left, preferred_element_type=jnp.float32)
    grad_flat_right = jnp.dot(edge_flat, mid_whole_right, preferred_element_type=jnp.float32)
    grad_left = grad_flat_left.astype(jnp.bfloat16).reshape(1, rows, depth, width)
    grad_right = grad_flat_right.astype(jnp.bfloat16).reshape(1, rows, depth, width)
    return (new_left[None], new_right[None], grad_left, grad_right)


def solution(mesh):
    placed = (
        P("site", "blk", None),
        P("site", "blk", None, None),
        P("site", "blk", None, None),
        P("site", "blk", None, None),
        P("site", None),
        P("site", "blk", None),
        P("site", "blk", None),
    )
    return jax.shard_map(
        body,
        mesh=mesh,
        in_specs=placed,
        out_specs=(
            P("site", "blk", None),
            P("site", "blk", None),
            P("site", "blk", None, None),
            P("site", "blk", None, None),
        ),
        check_vma=False,
    )
```

profile of v0, /device:TPU:0, one launch (start us, length us, event | category | flops | bytes accessed | tf_op | source)
XLA Modules:
  0.0 278.8 jit_solution(17810175746152495462)
XLA Ops:
  7.2 0.0 reduce-scatter.3.cloned.1.call-start
  7.2 13.9 %fusion.8 = f32[768,768]{1,0:T(8,128)} fusion(bf16[1,96,64,768]{3,2,1,0:T(8,128)(2,1)} %param.9, bf16[1,96,64,768]{3,2,1,0:T(8,128)(2,1)} %param.8), kind=kOutput, calls=%fused_computation.10 | convolution fusion | flops 7247757312 | bytes 21233664 | tf_op jit(solution)/shard_map/dot_general | solution.py:16
  21.1 0.0 reduce-scatter.3.cloned.1.call-update
  21.1 0.0 reduce-scatter.5.cloned.1.call-start
  21.2 13.9 %fusion.13 = f32[768,768]{1,0:T(8,128)} fusion(bf16[1,96,64,768]{3,2,1,0:T(8,128)(2,1)} %param.10, bf16[1,96,64,768]{3,2,1,0:T(8,128)(2,1)} %param.8), kind=kOutput, calls=%fused_computation.11 | convolution fusion | flops 7247757312 | bytes 21233664 | tf_op jit(solution)/shard_map/dot_general | solution.py:16
  35.1 0.0 reduce-scatter.5.cloned.1.call-update
  35.1 0.0 copy-start.9
  35.1 0.0 copy-start.8
  35.2 0.0 copy-start.3
  35.2 0.0 all-gather.7.cloned.1.call-start
  35.2 25.2 %reduce-scatter.3.cloned.1.call-done = f32[96,768]{1,0:T(8,128)} async-done(((f32[768,768]{1,0:T(8,128)}), f32[96,768]{1,0:T(8,128)}) %reduce-scatter.3.cloned.1.call-update) | async-done | bytes 294928 | tf_op jit(solution)/shard_map/reduce_scatter | solution.py:45
  60.4 1.6 convert_element_type.51
  62.0 0.0 all-gather.7.cloned.1.call-update
  62.0 0.0 copy-start.2
  62.1 0.0 all-gather.9.cloned.1.call-start
  62.1 36.5 %reduce-scatter.5.cloned.1.call-done = f32[96,768]{1,0:T(8,128)} async-done(((f32[768,768]{1,0:T(8,128)}), f32[96,768]{1,0:T(8,128)}) %reduce-scatter.5.cloned.1.call-update) | async-done | bytes 294928 | tf_op jit(solution)/shard_map/reduce_scatter | solution.py:46
  98.6 1.6 convert_element_type.53
  100.2 0.0 all-gather.9.cloned.1.call-update
  100.3 0.0 all-gather.13.cloned.1.call-start
  100.3 0.0 copy-done.9
  100.3 1.5 collective-permute-start
  101.8 4.6 %collective-permute-done = bf16[96,768]{1,0:T(8,128)(2,1)S(1)} collective-permute-done((bf16[96,768]{1,0:T(8,128)(2,1)S(1)}, bf16[96,768]{1,0:T(8,128)(2,1)S(1)}, u32[]{:S(2)}, u32[]{:S(2)}) %collective-permute-start) | collective-permute-done | bytes 147488 | tf_op jit(solution)/shard_map/ppermute | solution.py:12
  106.4 0.7 copy-done.4
  107.1 0.0 all-gather.13.cloned.1.call-update
  107.1 0.0 all-gather.11.cloned.1.call-start
  107.2 0.0 copy-done.8
  107.2 0.1 dynamic-slice_bitcast_fusion
  107.3 15.5 %all-gather.7.cloned.1.call-done = bf16[768,768]{1,0:T(8,128)(2,1)} async-done(((bf16[96,768]{1,0:T(8,128)(2,1)}), bf16[768,768]{1,0:T(8,128)(2,1)}) %all-gather.7.cloned.1.call-update) | async-done | bytes 1179664 | tf_op jit(solution)/shard_map/all_gather | solution.py:48
  122.8 0.0 copy-done.3
  122.8 1.8 fusion.36
  124.6 2.4 collective-permute-start.2
  127.0 20.3 %all-gather.9.cloned.1.call-done = bf16[768,768]{1,0:T(8,128)(2,1)} async-done(((bf16[96,768]{1,0:T(8,128)(2,1)}), bf16[768,768]{1,0:T(8,128)(2,1)}) %all-gather.9.cloned.1.call-update) | async-done | bytes 1179664 | tf_op jit(solution)/shard_map/all_gather | solution.py:49
  147.3 1.8 fusion.32
  149.1 1.5 collective-permute-start.4
  150.6 0.0 collective-permute-done.2
  150.6 0.5 fusion.34
  151.2 1.5 collective-permute-start.3
  152.7 7.2 %collective-permute-done.4 = f32[96,768]{1,0:T(8,128)S(1)} collective-permute-done((f32[96,768]{1,0:T(8,128)S(1)}, f32[96,768]{1,0:T(8,128)S(1)}, u32[]{:S(2)}, u32[]{:S(2)}) %collective-permute-start.4) | collective-permute-done | bytes 294944 | tf_op jit(solution)/shard_map/ppermute | solution.py:12
  159.9 0.5 fusion.30
  160.4 0.0 copy-start.10
  160.4 0.0 copy-start.5
  160.5 0.6 collective-permute-start.5
  161.1 5.2 %collective-permute-done.3 = f32[96,768]{1,0:T(8,128)S(1)} collective-permute-done((f32[96,768]{1,0:T(8,128)S(1)}, f32[96,768]{1,0:T(8,128)S(1)}, u32[]{:S(2)}, u32[]{:S(2)}) %collective-permute-start.3) | collective-permute-done | bytes 294944 | tf_op jit(solution)/shard_map/ppermute | solution.py:12
  166.2 5.6 %collective-permute-done.5 = f32[96,768]{1,0:T(8,128)S(1)} collective-permute-done((f32[96,768]{1,0:T(8,128)S(1)}, f32[96,768]{1,0:T(8,128)S(1)}, u32[]{:S(2)}, u32[]{:S(2)}) %collective-permute-start.5) | collective-permute-done | bytes 294944 | tf_op jit(solution)/shard_map/ppermute | solution.py:12
  171.8 0.8 fusion.29
  172.7 0.0 all-gather.11.cloned.1.call-update
  172.7 0.0 all-gather.17.cloned.1.call-start
  172.7 0.0 copy-done.10
  172.8 1.5 collective-permute-start.1
  174.3 3.7 %collective-permute-done.1 = bf16[96,768]{1,0:T(8,128)(2,1)S(1)} collective-permute-done((bf16[96,768]{1,0:T(8,128)(2,1)S(1)}, bf16[96,768]{1,0:T(8,128)(2,1)S(1)}, u32[]{:S(2)}, u32[]{:S(2)}) %collective-permute-start.1) | collective-permute-done | bytes 147488 | tf_op jit(solution)/shard_map/ppermute | solution.py:12
  178.0 0.7 copy-done.6
  178.6 0.0 all-gather.17.cloned.1.call-update
  178.7 0.0 copy-start.7
  178.7 0.2 all-gather.15.cloned.1.call-start
  178.9 1.0 fusion.22
  179.9 1.0 fusion.23
  180.9 0.0 all-gather.15.cloned.1.call-update
  180.9 0.0 all-gather.13.cloned.1.call-done
  181.0 15.3 %all-gather.11.cloned.1.call-done = bf16[768,768]{1,0:T(8,128)(2,1)} async-done(((bf16[96,768]{1,0:T(8,128)(2,1)}), bf16[768,768]{1,0:T(8,128)(2,1)}) %all-gather.11.cloned.1.call-update) | async-done | bytes 1179664 | tf_op jit(solution)/shard_map/all_gather | solution.py:71
  196.2 14.8 %fusion.6 = bf16[6144,768]{0,1:T(8,128)(2,1)} fusion(bf16[6144,768]{1,0:T(8,128)(2,1)} %bitcast.89, bf16[768,768]{1,0:T(8,128)(2,1)} %all-gather.11.cloned.1.call-done, bf16[768,768]{1,0:T(8,128)(2,1)} %all-gather.13.cloned.1.call-done), kind=kOutput, calls=%fused_computation.8 | convolution fusion | flops 8159035392 | bytes 21233664 | tf_op jit(solution)/shard_map/dot_general | solution.py:76
  211.0 12.6 %copy.21 = bf16[6144,768]{1,0:T(8,128)(2,1)} copy(bf16[6144,768]{0,1:T(8,128)(2,1)} %fusion.6) | data formatting | bytes 18874368 | tf_op jit(solution)/shard_map/convert_element_type | solution.py:78
  223.7 20.8 %all-gather.15.cloned.1.call-done = bf16[768,768]{1,0:T(8,128)(2,1)} async-done(((bf16[96,768]{1,0:T(8,128)(2,1)}), bf16[768,768]{1,0:T(8,128)(2,1)}) %all-gather.15.cloned.1.call-update) | async-done | bytes 1179664 | tf_op jit(solution)/shard_map/all_gather | solution.py:72
  244.4 14.9 %fusion.7 = bf16[6144,768]{0,1:T(8,128)(2,1)} fusion(bf16[6144,768]{1,0:T(8,128)(2,1)} %bitcast.90, bf16[768,768]{1,0:T(8,128)(2,1)} %all-gather.15.cloned.1.call-done, bf16[768,768]{1,0:T(8,128)(2,1)} %all-gather.17.cloned.1.call-done), kind=kOutput, calls=%fused_computation.9 | convolution fusion | flops 8159035392 | bytes 21233664 | tf_op jit(solution)/shard_map/dot_general | solution.py:77
  259.3 12.6 %copy.22 = bf16[6144,768]{1,0:T(8,128)(2,1)} copy(bf16[6144,768]{0,1:T(8,128)(2,1)} %fusion.7) | data formatting | bytes 18874368 | tf_op jit(solution)/shard_map/convert_element_type | solution.py:79
  (11 shorter events, 0.0 us)
Async XLA Ops:
  7.2 53.2 %reduce-scatter.3.cloned.1.call-start = ((), (), s32[]{:S(2)}) async-start(), calls=%async_computation.2 | async-start | bytes 2654208 | tf_op jit(solution)/shard_map/reduce_scatter | solution.py:45
  21.1 77.5 %reduce-scatter.5.cloned.1.call-start = ((), (), s32[]{:S(2)}) async-start(), calls=%async_computation.4 | async-start | bytes 2654208 | tf_op jit(solution)/shard_map/reduce_scatter | solution.py:46
  35.1 65.2 %copy-start.9 = (bf16[1,96,768]{2,1,0:T(8,128)(2,1)S(1)}, bf16[1,96,768]{2,1,0:T(8,128)(2,1)}, u32[]{:S(2)}) copy-start(bf16[1,96,768]{2,1,0:T(8,128)(2,1)} %param.7) | copy-start | bytes 442372
  35.1 72.0 %copy-start.8 = (s32[1,768]{1,0:T(1,128)S(1)}, s32[1,768]{1,0:T(1,128)}, u32[]{:S(2)}) copy-start(s32[1,768]{1,0:T(1,128)} %param.11) | copy-start | bytes 9220
  35.2 87.6 %copy-start.3 = (f32[1,96,768]{2,1,0:T(8,128)S(1)}, f32[1,96,768]{2,1,0:T(8,128)}, u32[]{:S(2)}) copy-start(f32[1,96,768]{2,1,0:T(8,128)} %param.12) | copy-start | bytes 884740
  35.2 87.6 %all-gather.7.cloned.1.call-start = ((), (), s32[]{:S(2)}) async-start(), calls=%async_computation.3 | async-start | bytes 1327104 | tf_op jit(solution)/shard_map/all_gather | solution.py:48
  62.0 85.3 %copy-start.2 = (f32[1,96,768]{2,1,0:T(8,128)S(1)}, f32[1,96,768]{2,1,0:T(8,128)}, u32[]{:S(2)}) copy-start(f32[1,96,768]{2,1,0:T(8,128)} %param.13) | copy-start | bytes 884740
  62.1 85.2 %all-gather.9.cloned.1.call-start = ((), (), s32[]{:S(2)}) async-start(), calls=%async_computation.5 | async-start | bytes 1327104 | tf_op jit(solution)/shard_map/all_gather | solution.py:49
  100.3 80.7 %all-gather.13.cloned.1.call-start = ((), (), s32[]{:S(2)}) async-start(), calls=%async_computation.7 | async-start | bytes 1327104 | tf_op jit(solution)/shard_map/all_gather | solution.py:69
  100.3 6.1 %collective-permute-start = (bf16[96,768]{1,0:T(8,128)(2,1)S(1)}, bf16[96,768]{1,0:T(8,128)(2,1)S(1)}, u32[]{:S(2)}, u32[]{:S(2)}) collective-permute-start(bf16[96,768]{1,0:T(8,128)(2,1)S(1)} %bitcast.91), channel_id=1, source_target_pairs={{24,0},{0,8},{8,16},{16,24},{25,1},{1,9},{9,17},{17,25},{26,2},{2,... | collective-permute-start | bytes 442376 | tf_op jit(solution)/shard_map/ppermute | solution.py:12
  106.4 0.7 copy-start.4
  107.1 89.1 %all-gather.11.cloned.1.call-start = ((), (), s32[]{:S(2)}) async-start(), calls=%async_computation.6 | async-start | bytes 1327104 | tf_op jit(solution)/shard_map/all_gather | solution.py:71
  124.6 26.1 %copy-start = (bf16[768,768]{1,0:T(8,128)(2,1)S(1)}, bf16[768,768]{1,0:T(8,128)(2,1)}, u32[]{:S(2)}) copy-start(bf16[768,768]{1,0:T(8,128)(2,1)} %all-gather.7.cloned.1.call-done) | copy-start | bytes 3538948
  124.6 26.1 %collective-permute-start.2 = (f32[96,768]{1,0:T(8,128)S(1)}, f32[96,768]{1,0:T(8,128)S(1)}, u32[]{:S(2)}, u32[]{:S(2)}) collective-permute-start(f32[96,768]{1,0:T(8,128)S(1)} %fusion.36), channel_id=1, source_target_pairs={{8,0},{16,8},{24,16},{0,24},{9,1},{17,9},{25,17},{1,25},{10,2},{18... | collective-permute-start | bytes 884744 | tf_op jit(solution)/shard_map/ppermute | solution.py:12
  149.1 10.8 %copy-start.1 = (bf16[768,768]{1,0:T(8,128)(2,1)S(1)}, bf16[768,768]{1,0:T(8,128)(2,1)}, u32[]{:S(2)}) copy-start(bf16[768,768]{1,0:T(8,128)(2,1)} %all-gather.9.cloned.1.call-done) | copy-start | bytes 3538948
  149.1 10.8 %collective-permute-start.4 = (f32[96,768]{1,0:T(8,128)S(1)}, f32[96,768]{1,0:T(8,128)S(1)}, u32[]{:S(2)}, u32[]{:S(2)}) collective-permute-start(f32[96,768]{1,0:T(8,128)S(1)} %fusion.32), channel_id=1, source_target_pairs={{24,0},{0,8},{8,16},{16,24},{25,1},{1,9},{9,17},{17,25},{26,2},{2,... | collective-permute-start | bytes 884744 | tf_op jit(solution)/shard_map/ppermute | solution.py:12
  151.2 15.1 %collective-permute-start.3 = (f32[96,768]{1,0:T(8,128)S(1)}, f32[96,768]{1,0:T(8,128)S(1)}, u32[]{:S(2)}, u32[]{:S(2)}) collective-permute-start(f32[96,768]{1,0:T(8,128)S(1)} %fusion.34), channel_id=1, source_target_pairs={{8,0},{16,8},{24,16},{0,24},{9,1},{17,9},{25,17},{1,25},{10,2},{18... | collective-permute-start | bytes 884744 | tf_op jit(solution)/shard_map/ppermute | solution.py:12
  160.4 12.3 %copy-start.10 = (bf16[1,96,768]{2,1,0:T(8,128)(2,1)S(1)}, bf16[1,96,768]{2,1,0:T(8,128)(2,1)}, u32[]{:S(2)}) copy-start(bf16[1,96,768]{2,1,0:T(8,128)(2,1)} %param.7) | copy-start | bytes 442372
  160.4 18.5 %copy-start.5 = (bf16[96,768]{1,0:T(8,128)(2,1)S(1)}, bf16[96,768]{1,0:T(8,128)(2,1)}, u32[]{:S(2)}) copy-start(bf16[96,768]{1,0:T(8,128)(2,1)} %copy-done.4) | copy-start | bytes 442372
  160.5 11.4 %collective-permute-start.5 = (f32[96,768]{1,0:T(8,128)S(1)}, f32[96,768]{1,0:T(8,128)S(1)}, u32[]{:S(2)}, u32[]{:S(2)}) collective-permute-start(f32[96,768]{1,0:T(8,128)S(1)} %fusion.30), channel_id=1, source_target_pairs={{24,0},{0,8},{8,16},{16,24},{25,1},{1,9},{9,17},{17,25},{26,2},{2,... | collective-permute-start | bytes 884744 | tf_op jit(solution)/shard_map/ppermute | solution.py:12
  172.7 51.0 %all-gather.17.cloned.1.call-start = ((), (), s32[]{:S(2)}) async-start(), calls=%async_computation.9 | async-start | bytes 1327104 | tf_op jit(solution)/shard_map/all_gather | solution.py:70
  172.8 5.2 %collective-permute-start.1 = (bf16[96,768]{1,0:T(8,128)(2,1)S(1)}, bf16[96,768]{1,0:T(8,128)(2,1)S(1)}, u32[]{:S(2)}, u32[]{:S(2)}) collective-permute-start(bf16[96,768]{1,0:T(8,128)(2,1)S(1)} %bitcast.92), channel_id=1, source_target_pairs={{8,0},{16,8},{24,16},{0,24},{9,1},{17,9},{25,17},{1,25},{10,2},{18... | collective-permute-start | bytes 442376 | tf_op jit(solution)/shard_map/ppermute | solution.py:12
  178.0 0.7 copy-start.6
  178.7 1.3 copy-start.7
  178.7 65.7 %all-gather.15.cloned.1.call-start = ((), (), s32[]{:S(2)}) async-start(), calls=%async_computation.8 | async-start | bytes 1327104 | tf_op jit(solution)/shard_map/all_gather | solution.py:72
Sparse Core Ops, SparseCore 0:
  21.3 39.0 reduce-scatter.2
  63.3 35.2 reduce-scatter.4
  100.8 21.9 all-gather.6
  124.8 22.4 all-gather.8
  149.4 22.4 all-gather.12
  173.9 22.2 all-gather.10
  197.9 22.4 all-gather.16
  222.0 22.4 all-gather.14
where the time goes:
time: 280 us; the launch traced here: 279 us
  waiting for transfers between devices  160 us (57%)
  matrix products  64.2 us (23%)
  local copies, waits for them, and re-layouts  26.7 us (10%)
  between operations  14.3 us (5%)
  starting transfers between devices  9.61 us (3%)
  other arithmetic  4.11 us (1%)
    reduce_scatter x1, waiting for transfers between devices, body(): lax.psum_scatter(partial_term(right_flat), 'blk', scatter_dimension=0, ti...  36.5 us
    dot_general x2, matrix products, contract_first(): lax.dot_general(left, right, (((0,), (0,)), ((), ())), preferred_element_...  27.8 us
    ppermute x6, waiting for transfers between devices, shifted(): return lax.ppermute(block, axis, route)  26.3 us
    reduce_scatter x1, waiting for transfers between devices, body(): lax.psum_scatter(partial_term(left_flat), 'blk', scatter_dimension=0, til...  25.2 us
    all_gather x1, waiting for transfers between devices, body(): lax.all_gather(w_right, 'blk', axis=0, tiled=True)  20.8 us
    all_gather x1, waiting for transfers between devices, body(): lax.all_gather(part_right.astype(jnp.bfloat16), 'blk', axis=0, tiled=True)  20.3 us
    all_gather x1, waiting for transfers between devices, body(): lax.all_gather(part_left.astype(jnp.bfloat16), 'blk', axis=0, tiled=True)  15.5 us
    all_gather x1, waiting for transfers between devices, body(): lax.all_gather(w_left, 'blk', axis=0, tiled=True)  15.3 us
  transfers between devices with their start and end apart: 14, of which 11 were waited for; matrix products, arithmetic and copies ran while one was open for 19% of the time, Pallas kernels for 0%

commit v1 on v0

v1 whole, which is shorter than its diff:
```python
import functools

import jax
import jax.numpy as jnp
from jax import lax
from jax.experimental import pallas as pl
from jax.experimental.pallas import tpu as pltpu
from jax.sharding import PartitionSpec as P

ITERS = 2
LANES = 128
STEPS = 8
F32 = jnp.float32
BF16 = jnp.bfloat16


def dot(left, right, dims):
    return lax.dot_general(left, right, (dims, ((), ())), preferred_element_type=F32)


def chain_kernel(
    nsite, nblk, steps,
    corner, edge, left, right, labels, cot_left, cot_right,
    mids, new_left, new_right,
    acc, snd, rcv, enl, cland, cfull, lab_in, lab_dst, col_own, col_dst, cotf, wsend, cpair,
    wzero, wfull, part, got, newp, newgot, mid_got,
    c_s, c_r, l_s, l_r, w_s, w_r, p_s, p_r, e_s, e_r, r_s, r_r, a_s, a_r, n_s, n_r, m_s, m_r,
):
    step = pl.program_id(0)
    rows, width = corner.shape
    nz = nblk // 2
    pair = 2 * rows
    aligned = rows % 16 == 0
    blocks = width // LANES
    site = lax.axis_index("site")
    blk = lax.axis_index("blk")
    side = blk % 2
    z = blk // 2
    up = (site + 1) % nsite
    down = (site + nsite - 1) % nsite
    dest = (site + nsite - 1 + 2 * side) % nsite
    origin = (site + nsite + 1 - 2 * side) % nsite
    partner = 2 * z + 1 - side

    def copy(src, dst, send, recv, to_site, to_blk):
        return pltpu.make_async_remote_copy(
            src_ref=src, dst_ref=dst, send_sem=send, recv_sem=recv,
            device_id={"site": to_site, "blk": to_blk}, device_id_type=pl.DeviceIdType.MESH,
        )

    def own_rows(index):
        return pl.ds(pl.multiple_of(index * rows, rows), rows)

    def pair_rows(index):
        return pl.ds(pl.multiple_of(index * pair, pair), pair)

    def corner_slot(index):
        return cfull.at[own_rows(index)] if aligned else cland.at[index]

    def corner_copies():
        there = corner_slot(blk)
        out = []
        for p in range(nz):
            out.append(copy(corner, there, c_s.at[0, p], c_r.at[blk], up, 2 * p))
            out.append(copy(corner, there, c_s.at[1, p], c_r.at[blk], down, 2 * p + 1))
        return out

    def w_copies():
        out = []
        for d in range(1, nblk):
            to = (blk + d) % nblk
            out.append(copy(wsend.at[to % 2], wzero.at[own_rows(blk)], w_s.at[d], w_r.at[blk], site, to))
        return out

    def label_copy():
        return copy(lab_in, lab_dst, l_s, l_r, origin, blk)

    def cot_copy():
        return copy(cotf.at[1 - side], cpair.at[own_rows(side)], p_s, p_r, site, partner)

    def columns(lab, col):
        for i in range(blocks):
            at = slice(i * LANES, (i + 1) * LANES)
            col[at, :] = jnp.broadcast_to(lab[0:1, at].astype(F32), (LANES, LANES)).T

    def same(col_block, lab, j):
        return col_block == lab[0:1, j * LANES:(j + 1) * LANES].astype(F32)

    @pl.when(step == 0)
    def _():
        barrier = pltpu.get_barrier_semaphore()
        for where in (down, up):
            for b in range(nblk):
                pl.semaphore_signal(barrier, inc=1, device_id={"site": where, "blk": b}, device_id_type=pl.DeviceIdType.MESH)
        for d in range(1, nblk):
            pl.semaphore_signal(barrier, inc=1, device_id={"site": site, "blk": (blk + d) % nblk}, device_id_type=pl.DeviceIdType.MESH)
        pl.semaphore_wait(barrier, 3 * nblk - 1)
        lab_in[...] = labels[...]
        label_copy().start()
        columns(labels, col_own)
        mine = col_own[own_rows(blk), :]
        for s, cot in enumerate((cot_left, cot_right)):
            total = jnp.zeros((rows, LANES), F32)
            for j in range(blocks):
                total = total + jnp.where(same(mine, labels, j), cot[:, j * LANES:(j + 1) * LANES], 0.0)
            cotf[s] = total
            wsend[s] = total.astype(BF16).astype(wsend.dtype)
        cot_copy().start()
        for c in w_copies():
            c.start()
        for c in corner_copies():
            c.start()
        wzero[own_rows(blk), :] = wsend[side]
        cpair[own_rows(side), :] = cotf[side]
        acc[...] = jnp.zeros_like(acc)

    acc[0] += dot(edge[...], left[...], ((0,), (0,)))
    acc[1] += dot(edge[...], right[...], ((0,), (0,)))

    def window(i):
        return max(0, i - 1), min(blocks, i + 2)

    def back_partial(at):
        for i in range(blocks):
            rows_i = slice(i * LANES, (i + 1) * LANES)
            lo, hi = window(i)
            span = slice(lo * LANES, hi * LANES)
            folded = wzero[rows_i, :] if at == 0 else wfull[at - 1, rows_i, :]
            mine = col_own[rows_i, :]
            there = col_dst[rows_i, :]
            w = jnp.concatenate(
                [jnp.where(same(mine, labels, j), folded.astype(F32), 0.0) for j in range(lo, hi)], axis=1
            ).astype(BF16)
            back = dot(w, enl[span, span], ((1,), (1,)))
            total = jnp.zeros((LANES, LANES), F32)
            for j in range(lo, hi):
                piece = back[:, (j - lo) * LANES:(j - lo + 1) * LANES]
                total = total + jnp.where(same(there, lab_dst, j), piece, 0.0)
            part[at, rows_i, :] = total.astype(BF16)

    def reduce_copies(at):
        return [
            copy(part.at[at, slice_of(p)], got.at[at, z], r_s.at[at, p], r_r.at[at, z], dest, 2 * p + side)
            for p in range(nz)
        ]

    def slice_of(p):
        return pl.ds(p * pair, pair)

    def gather_copies(at):
        here = wfull.at[at, pair_rows(z)]
        return [
            copy(here, here, a_s.at[at, d], a_r.at[at, z], site, 2 * ((z + d) % nz) + side)
            for d in range(1, nz)
        ]

    def reduce_and_send(at):
        for q in range(nz):
            copy(got.at[at, q], got.at[at, q], r_s.at[at, q], r_r.at[at, q], dest, blk).wait_recv()
        total = cpair[...]
        for q in range(nz):
            total = total + got[at, q].astype(F32)
        wfull[at, pair_rows(z), :] = total.astype(BF16)
        for c in gather_copies(at):
            c.start()

    def gather_wait(at):
        for d in range(1, nz):
            src = (z + nz - d) % nz
            there = wfull.at[at, pair_rows(src)]
            copy(there, there, a_s.at[at, d], a_r.at[at, src], site, partner).wait_recv()

    def new_copies():
        out = []
        for d in range(1, nblk):
            to = (blk + d) % nblk
            out.append(copy(newp.at[own_rows(to)], newgot.at[blk], n_s.at[d], n_r.at[blk], site, to))
        return out

    @pl.when(step == steps - 1)
    def _():
        snd[...] = acc[1 - side].astype(BF16)
        swap = copy(snd, rcv, e_s, e_r, site, partner)
        swap.start()
        label_copy().wait_recv()
        columns(lab_dst, col_dst)
        cot_copy().wait_recv()
        for d in range(1, nblk):
            src = (blk + nblk - d) % nblk
            there = wzero.at[own_rows(src)]
            copy(there, there, w_s.at[d], w_r.at[src], site, partner).wait_recv()
        swap.wait_recv()
        enl[...] = (acc[side] + rcv[...].astype(F32)).astype(BF16)
        back_partial(0)
        for c in reduce_copies(0):
            c.start()
        for q in range(nblk):
            there = corner_slot(q)
            copy(there, there, c_s.at[0, 0], c_r.at[q], site, partner).wait_recv()
        if not aligned:
            for q in range(nz):
                both = [cland[2 * q].astype(F32), cland[2 * q + 1].astype(F32)]
                cfull[q * pair:(q + 1) * pair, :] = jnp.concatenate(both, axis=0).astype(BF16)
        for i in range(blocks):
            rows_i = slice(i * LANES, (i + 1) * LANES)
            lo, hi = window(i)
            fresh = dot(cfull[rows_i, :], enl[:, lo * LANES:hi * LANES], ((1,), (0,)))
            mine = col_own[rows_i, :]
            total = jnp.zeros((LANES, LANES), F32)
            for j in range(lo, hi):
                piece = fresh[:, (j - lo) * LANES:(j - lo + 1) * LANES]
                total = total + jnp.where(same(mine, labels, j), piece, 0.0)
            newp[rows_i, :] = total.astype(newp.dtype)
        reduce_and_send(0)
        for c in new_copies():
            c.start()
        newgot[blk] = newp[own_rows(blk), :]
        for at in range(1, ITERS):
            gather_wait(at - 1)
            back_partial(at)
            for c in reduce_copies(at):
                c.start()
            reduce_and_send(at)
        for d in range(1, nblk):
            src = (blk + nblk - d) % nblk
            copy(newgot.at[src], newgot.at[src], n_s.at[d], n_r.at[src], site, partner).wait_recv()
        mine = col_own[own_rows(blk), :]
        for s, out in enumerate((new_left, new_right)):
            total = jnp.zeros((rows, LANES), F32)
            for q in range(nz):
                total = total + newgot[2 * q + s].astype(F32)
            for j in range(blocks):
                out[:, j * LANES:(j + 1) * LANES] = jnp.where(same(mine, labels, j), total, 0.0).astype(BF16)
        gather_wait(ITERS - 1)
        for j in range(blocks):
            lo, hi = window(j)
            span = slice(lo * LANES, hi * LANES)
            w = jnp.where(same(col_own[span, :], labels, j), wfull[ITERS - 1, span, :].astype(F32), 0.0).astype(BF16)
            snd2 = dot(cfull[span, :], w, ((0,), (0,))).astype(BF16)
            mids[side, :, j * LANES:(j + 1) * LANES] = snd2
            enl[:, j * LANES:(j + 1) * LANES] = snd2
        last = copy(enl, mid_got, m_s, m_r, site, partner)
        last.start()
        last.wait_recv()
        mids[1 - side] = mid_got[...]
        last.wait_send()
        swap.wait_send()
        label_copy().wait_send()
        cot_copy().wait_send()
        for c in w_copies() + corner_copies() + new_copies():
            c.wait_send()
        for at in range(ITERS):
            for c in reduce_copies(at) + gather_copies(at):
                c.wait_send()


def grad_kernel(edge, mids, grad_left, grad_right):
    grad_left[...] = dot(edge[...], mids[0], ((1,), (0,))).astype(BF16)
    grad_right[...] = dot(edge[...], mids[1], ((1,), (0,))).astype(BF16)


def body(nsite, nblk, corner, edge, proj_left, proj_right, charge, cot_left, cot_right):
    rows, width = corner.shape[1:]
    depth = edge.shape[2]
    nz = nblk // 2
    pair = 2 * rows
    deep = rows * depth
    chunk = deep // STEPS
    edge_flat = edge[0].reshape(deep, width)
    left_flat = proj_left[0].reshape(deep, width)
    right_flat = proj_right[0].reshape(deep, width)
    labels = jnp.broadcast_to(charge, (8, width))

    def whole(*shape):
        return pl.BlockSpec(shape, lambda k: (0,) * len(shape))

    def piece():
        return pl.BlockSpec((chunk, width), lambda k: (k, 0))

    aligned = rows % 16 == 0
    small = BF16 if aligned else F32
    dma = pltpu.SemaphoreType.DMA
    mids, new_left, new_right = pl.pallas_call(
        functools.partial(chain_kernel, nsite, nblk, STEPS),
        grid=(STEPS,),
        out_shape=(
            jax.ShapeDtypeStruct((2, width, width), BF16),
            jax.ShapeDtypeStruct((rows, width), BF16),
            jax.ShapeDtypeStruct((rows, width), BF16),
        ),
        in_specs=[
            whole(rows, width), piece(), piece(), piece(), whole(8, width),
            whole(rows, width), whole(rows, width),
        ],
        out_specs=(whole(2, width, width), whole(rows, width), whole(rows, width)),
        scratch_shapes=[
            pltpu.VMEM((2, width, width), F32),
            pltpu.VMEM((width, width), BF16),
            pltpu.VMEM((width, width), BF16),
            pltpu.VMEM((width, width), BF16),
            pltpu.VMEM((1, 16, LANES) if aligned else (nblk, rows, width), BF16),
            pltpu.VMEM((width, width), BF16),
            pltpu.VMEM((8, width), jnp.int32),
            pltpu.VMEM((8, width), jnp.int32),
            pltpu.VMEM((width, LANES), F32),
            pltpu.VMEM((width, LANES), F32),
            pltpu.VMEM((2, rows, LANES), F32),
            pltpu.VMEM((2, rows, LANES), small),
            pltpu.VMEM((pair, LANES), F32),
            pltpu.VMEM((width, LANES), small),
            pltpu.VMEM((ITERS, width, LANES), BF16),
            pltpu.VMEM((ITERS, width, LANES), BF16),
            pltpu.VMEM((ITERS, nz, pair, LANES), BF16),
            pltpu.VMEM((width, LANES), small),
            pltpu.VMEM((nblk, rows, LANES), small),
            pltpu.VMEM((width, width), BF16),
            dma((2, nz)), dma((nblk,)),
            dma(()), dma(()),
            dma((nblk,)), dma((nblk,)),
            dma(()), dma(()),
            dma(()), dma(()),
            dma((ITERS, nz)), dma((ITERS, nz)),
            dma((ITERS, nz)), dma((ITERS, nz)),
            dma((nblk,)), dma((nblk,)),
            dma(()), dma(()),
        ],
        compiler_params=pltpu.CompilerParams(
            collective_id=0, has_side_effects=True, vmem_limit_bytes=52 * 1024 * 1024,
            dimension_semantics=("arbitrary",),
        ),
    )(corner[0], edge_flat, left_flat, right_flat, labels, cot_left[0], cot_right[0])
    grad_left, grad_right = pl.pallas_call(
        grad_kernel,
        grid=(STEPS,),
        out_shape=(jax.ShapeDtypeStruct((deep, width), BF16),) * 2,
        in_specs=[piece(), whole(2, width, width)],
        out_specs=(piece(), piece()),
        compiler_params=pltpu.CompilerParams(
            vmem_limit_bytes=48 * 1024 * 1024, dimension_semantics=("arbitrary",)
        ),
    )(edge_flat, mids)
    shape = (1, rows, depth, width)
    return (new_left[None], new_right[None], grad_left.reshape(shape), grad_right.reshape(shape))


def solution(mesh):
    placed = (
        P("site", "blk", None),
        P("site", "blk", None, None),
        P("site", "blk", None, None),
        P("site", "blk", None, None),
        P("site", None),
        P("site", "blk", None),
        P("site", "blk", None),
    )
    return jax.shard_map(
        functools.partial(body, mesh.shape["site"], mesh.shape["blk"]),
        mesh=mesh,
        in_specs=placed,
        out_specs=(
            P("site", "blk", None),
            P("site", "blk", None),
            P("site", "blk", None, None),
            P("site", "blk", None, None),
        ),
        check_vma=False,
    )
```

time: 280 us -> 97.6 us (0.35)
  waiting for transfers between devices: 160 us -> 0 us
  Pallas kernels: 0 us -> 90 us
  matrix products: 64.2 us -> 0 us
  local copies, waits for them, and re-layouts: 26.7 us -> 5.81 us
  between operations: 14.3 us -> 0.67 us
  starting transfers between devices: 9.61 us -> 0 us
  other arithmetic: 4.11 us -> 0.7 us
    pallas_call x0 -> x2, Pallas kernels: none -> 90 us  [the longest x1 71.3 us: body(): pl.pallas_call(functools.partial(chain_kernel, nsite, nblk, STEPS), grid=...]
    all_gather x6 -> x0, waiting for transfers between devices: 71.9 us -> none  [the longest x1 20.8 us: body(): lax.all_gather(w_right, 'blk', axis=0, tiled=True)]
    dot_general x10 -> x0, matrix products: 64.2 us -> none  [the longest x2 27.8 us: contract_first(): lax.dot_general(left, right, (((0,), (0,)), ((), ())), preferred_element_...]
    reduce_scatter x2 -> x0, waiting for transfers between devices: 61.7 us -> none  [the longest x1 36.5 us: body(): lax.psum_scatter(partial_term(right_flat), 'blk', scatter_dimension=0, ti...]
    ppermute x6 -> x0, waiting for transfers between devices: 26.3 us -> none  [shifted(): return lax.ppermute(block, axis, route)]
    convert_element_type x2 -> x0, local copies, waits for them, and re-layouts: 25.2 us -> none  [the longest x1 12.6 us: body(): grad_flat_left.astype(jnp.bfloat16).reshape(1, rows, depth, width)]
    ppermute x6 -> x0, starting transfers between devices: 9.1 us -> none  [shifted(): return lax.ppermute(block, axis, route)]
    unnamed x22 -> x10, local copies, waits for them, and re-layouts: 1.38 us -> 5.81 us
  transfers between devices with their start and end apart: 14 -> 0, of which waited for: 11 -> 0; matrix products, arithmetic and copies ran while one was open for 19% -> 0% of each run, Pallas kernels for 0% -> 0%
where the time goes in v1:
time: 97.6 us; the launch traced here: 97.1 us
  Pallas kernels  90 us (92%)
  local copies, waits for them, and re-layouts  5.81 us (6%)
    pallas_call x1, Pallas kernels, body(): pl.pallas_call(functools.partial(chain_kernel, nsite, nblk, STEPS), grid=...  71.3 us
    pallas_call x1, Pallas kernels, body(): pl.pallas_call(grad_kernel, grid=(STEPS,), out_shape=(jax.ShapeDtypeStruc...  18.6 us
    unnamed x10, local copies, waits for them, and re-layouts  5.81 us

profile of v1, /device:TPU:0, one launch (start us, length us, event | category | flops | bytes accessed | tf_op | source)
XLA Modules:
  0.0 97.1 jit_solution(16319108054412078644)
XLA Ops:
  0.6 0.7 reduce
  1.3 0.0 copy-start.1
  1.4 1.0 copy-done.1
  2.3 0.0 copy-start.2
  2.3 1.0 copy-done.2
  3.3 0.0 copy-start.3
  3.3 0.9 copy-done.3
  4.2 71.3 %shard_map.102 = (bf16[2,768,768]{2,1,0:T(8,128)(2,1)}, bf16[96,768]{1,0:T(8,128)(2,1)S(1)}, bf16[96,768]{1,0:T(8,128)(2,1)S(1)}) custom-call(bf16[96,768]{1,0:T(8,128)(2,1)S(1)} %bitcast.12, bf16[6144,768]{1,0:T(8,128)(2,1)} %bitcast.15, bf16[6144,768]{1,0:T(8,128)(2,1)} %bitcast.17, bf16[6144,768]{1,0:T(8,128)(2,1)} %bitcast.18, ...), custom_call_target="tpu_custom_call" | custom-call | tf_op jit(solution)/shard_map/pallas_call | solution.py:283
  75.5 0.0 copy-start
  75.5 1.7 %copy-done = bf16[2,768,768]{2,1,0:T(8,128)(2,1)S(1)} copy-done((bf16[2,768,768]{2,1,0:T(8,128)(2,1)S(1)}, bf16[2,768,768]{2,1,0:T(8,128)(2,1)}, u32[]{:S(2)}) %copy-start) | copy-done | bytes 2359320
  77.2 18.6 %shard_map.103 = (bf16[6144,768]{1,0:T(8,128)(2,1)}, bf16[6144,768]{1,0:T(8,128)(2,1)}) custom-call(bf16[6144,768]{1,0:T(8,128)(2,1)} %bitcast.16, bf16[2,768,768]{2,1,0:T(8,128)(2,1)S(1)} %copy-done), custom_call_target="tpu_custom_call" | custom-call | tf_op jit(solution)/shard_map/pallas_call | solution.py:332
  95.8 0.7 copy.13
  96.5 0.7 copy.14
  (1 shorter events, 0.0 us)
Async XLA Ops:
  1.3 1.0 copy-start.1
  2.3 1.0 copy-start.2
  3.3 0.9 copy-start.3
  75.5 1.7 %copy-start = (bf16[2,768,768]{2,1,0:T(8,128)(2,1)S(1)}, bf16[2,768,768]{2,1,0:T(8,128)(2,1)}, u32[]{:S(2)}) copy-start(bf16[2,768,768]{2,1,0:T(8,128)(2,1)} %get-tuple-element.11.mids) | copy-start | bytes 7077892

commit v2 on v1

--- a/solution.py
+++ b/solution.py
@@ -9,7 +9,7 @@
 
 ITERS = 2
 LANES = 128
-STEPS = 8
+VMEM = 60 * 1024 * 1024
 F32 = jnp.float32
 BF16 = jnp.bfloat16
 
@@ -21,15 +21,16 @@
 def chain_kernel(
     nsite, nblk, steps,
     corner, edge, left, right, labels, cot_left, cot_right,
-    mids, new_left, new_right,
-    acc, snd, rcv, enl, cland, cfull, lab_in, lab_dst, col_own, col_dst, cotf, wsend, cpair,
+    mids, fresh_out,
+    ebuf, pbuf, acc, snd, rcv, enl, cland, cfull, lab_in, lab_dst, col_own, col_dst, cotf, wsend, cpair,
     wzero, wfull, part, got, newp, newgot, mid_got,
-    c_s, c_r, l_s, l_r, w_s, w_r, p_s, p_r, e_s, e_r, r_s, r_r, a_s, a_r, n_s, n_r, m_s, m_r,
+    f_s, c_s, c_r, l_s, l_r, w_s, w_r, p_s, p_r, e_s, e_r, r_s, r_r, a_s, a_r, n_s, n_r, m_s, m_r,
 ):
     step = pl.program_id(0)
     rows, width = corner.shape
     nz = nblk // 2
     pair = 2 * rows
+    chunk = edge.shape[0]
     aligned = rows % 16 == 0
     blocks = width // LANES
     site = lax.axis_index("site")
@@ -86,36 +87,69 @@
     def same(col_block, lab, j):
         return col_block == lab[0:1, j * LANES:(j + 1) * LANES].astype(F32)
 
+    def fetch(t):
+        use_left = (t < steps) == (side == 1)
+        here = pl.ds(pl.multiple_of(t % steps * chunk, chunk), chunk)
+
+        @pl.when(use_left)
+        def _():
+            pltpu.make_async_copy(left.at[here], pbuf.at[t % 3], f_s.at[t % 3]).start()
+
+        @pl.when(jnp.logical_not(use_left))
+        def _():
+            pltpu.make_async_copy(right.at[here], pbuf.at[t % 3], f_s.at[t % 3]).start()
+
     @pl.when(step == 0)
     def _():
+        fetch(step)
+        fetch(step + 1)
         barrier = pltpu.get_barrier_semaphore()
         for where in (down, up):
             for b in range(nblk):
                 pl.semaphore_signal(barrier, inc=1, device_id={"site": where, "blk": b}, device_id_type=pl.DeviceIdType.MESH)
         for d in range(1, nblk):
             pl.semaphore_signal(barrier, inc=1, device_id={"site": site, "blk": (blk + d) % nblk}, device_id_type=pl.DeviceIdType.MESH)
-        pl.semaphore_wait(barrier, 3 * nblk - 1)
-        lab_in[...] = labels[...]
-        label_copy().start()
-        columns(labels, col_own)
+        lab_in[...] = jnp.broadcast_to(labels[...], lab_in.shape)
+        columns(lab_in, col_own)
         mine = col_own[own_rows(blk), :]
         for s, cot in enumerate((cot_left, cot_right)):
             total = jnp.zeros((rows, LANES), F32)
             for j in range(blocks):
-                total = total + jnp.where(same(mine, labels, j), cot[:, j * LANES:(j + 1) * LANES], 0.0)
+                total = total + jnp.where(same(mine, lab_in, j), cot[:, j * LANES:(j + 1) * LANES], 0.0)
             cotf[s] = total
             wsend[s] = total.astype(BF16).astype(wsend.dtype)
-        cot_copy().start()
-        for c in w_copies():
-            c.start()
-        for c in corner_copies():
-            c.start()
         wzero[own_rows(blk), :] = wsend[side]
         cpair[own_rows(side), :] = cotf[side]
         acc[...] = jnp.zeros_like(acc)
 
-    acc[0] += dot(edge[...], left[...], ((0,), (0,)))
-    acc[1] += dot(edge[...], right[...], ((0,), (0,)))
+    @pl.when(step == 1)
+    def _():
+        pl.semaphore_wait(pltpu.get_barrier_semaphore(), 3 * nblk - 1)
+        label_copy().start()
+        cot_copy().start()
+        for c in w_copies() + corner_copies():
+            c.start()
+
+    @pl.when(step + 2 < 2 * steps)
+    def _():
+        fetch(step + 2)
+
+    pltpu.make_async_copy(left.at[pl.ds(0, chunk)], pbuf.at[step % 3], f_s.at[step % 3]).wait()
+
+    @pl.when(step < steps)
+    def _():
+        turned = edge[...].T
+        ebuf[step] = turned
+        acc[0] += dot(turned, pbuf[step % 3], ((1,), (0,)))
+
+    @pl.when(step == steps)
+    def _():
+        snd[...] = acc[0].astype(BF16)
+        copy(snd, rcv, e_s, e_r, site, partner).start()
+
+    @pl.when(step >= steps)
+    def _():
+        acc[1] += dot(ebuf[step - steps], pbuf[step % 3], ((1,), (0,)))
 
     def window(i):
         return max(0, i - 1), min(blocks, i + 2)
@@ -129,7 +163,7 @@
             mine = col_own[rows_i, :]
             there = col_dst[rows_i, :]
             w = jnp.concatenate(
-                [jnp.where(same(mine, labels, j), folded.astype(F32), 0.0) for j in range(lo, hi)], axis=1
+                [jnp.where(same(mine, lab_in, j), folded.astype(F32), 0.0) for j in range(lo, hi)], axis=1
             ).astype(BF16)
             back = dot(w, enl[span, span], ((1,), (1,)))
             total = jnp.zeros((LANES, LANES), F32)
@@ -177,23 +211,7 @@
             out.append(copy(newp.at[own_rows(to)], newgot.at[blk], n_s.at[d], n_r.at[blk], site, to))
         return out
 
-    @pl.when(step == steps - 1)
-    def _():
-        snd[...] = acc[1 - side].astype(BF16)
-        swap = copy(snd, rcv, e_s, e_r, site, partner)
-        swap.start()
-        label_copy().wait_recv()
-        columns(lab_dst, col_dst)
-        cot_copy().wait_recv()
-        for d in range(1, nblk):
-            src = (blk + nblk - d) % nblk
-            there = wzero.at[own_rows(src)]
-            copy(there, there, w_s.at[d], w_r.at[src], site, partner).wait_recv()
-        swap.wait_recv()
-        enl[...] = (acc[side] + rcv[...].astype(F32)).astype(BF16)
-        back_partial(0)
-        for c in reduce_copies(0):
-            c.start()
+    def corner_wait():
         for q in range(nblk):
             there = corner_slot(q)
             copy(there, there, c_s.at[0, 0], c_r.at[q], site, partner).wait_recv()
@@ -201,6 +219,8 @@
             for q in range(nz):
                 both = [cland[2 * q].astype(F32), cland[2 * q + 1].astype(F32)]
                 cfull[q * pair:(q + 1) * pair, :] = jnp.concatenate(both, axis=0).astype(BF16)
+
+    def new_partial():
         for i in range(blocks):
             rows_i = slice(i * LANES, (i + 1) * LANES)
             lo, hi = window(i)
@@ -209,44 +229,64 @@
             total = jnp.zeros((LANES, LANES), F32)
             for j in range(lo, hi):
                 piece = fresh[:, (j - lo) * LANES:(j - lo + 1) * LANES]
-                total = total + jnp.where(same(mine, labels, j), piece, 0.0)
+                total = total + jnp.where(same(mine, lab_in, j), piece, 0.0)
             newp[rows_i, :] = total.astype(newp.dtype)
-        reduce_and_send(0)
-        for c in new_copies():
-            c.start()
-        newgot[blk] = newp[own_rows(blk), :]
-        for at in range(1, ITERS):
-            gather_wait(at - 1)
+
+    def mid_copy(j):
+        here = slice(j * LANES, (j + 1) * LANES)
+        return copy(enl.at[:, here], mid_got.at[:, here], m_s.at[j], m_r.at[j], site, partner)
+
+    @pl.when(step == 2 * steps - 1)
+    def _():
+        label_copy().wait_recv()
+        columns(lab_dst, col_dst)
+        cot_copy().wait_recv()
+        for d in range(1, nblk):
+            src = (blk + nblk - d) % nblk
+            there = wzero.at[own_rows(src)]
+            copy(there, there, w_s.at[d], w_r.at[src], site, partner).wait_recv()
+        swap = copy(snd, rcv, e_s, e_r, site, partner)
+        swap.wait_recv()
+        enl[...] = (acc[1] + rcv[...].astype(F32)).astype(BF16)
+        for at in range(ITERS):
+            if at:
+                gather_wait(at - 1)
             back_partial(at)
             for c in reduce_copies(at):
                 c.start()
+            if at == ITERS - 1:
+                corner_wait()
+                new_partial()
+                for c in new_copies():
+                    c.start()
+                newgot[blk] = newp[own_rows(blk), :]
             reduce_and_send(at)
-        for d in range(1, nblk):
-            src = (blk + nblk - d) % nblk
-            copy(newgot.at[src], newgot.at[src], n_s.at[d], n_r.at[src], site, partner).wait_recv()
-        mine = col_own[own_rows(blk), :]
-        for s, out in enumerate((new_left, new_right)):
-            total = jnp.zeros((rows, LANES), F32)
-            for q in range(nz):
-                total = total + newgot[2 * q + s].astype(F32)
-            for j in range(blocks):
-                out[:, j * LANES:(j + 1) * LANES] = jnp.where(same(mine, labels, j), total, 0.0).astype(BF16)
         gather_wait(ITERS - 1)
         for j in range(blocks):
             lo, hi = window(j)
             span = slice(lo * LANES, hi * LANES)
-            w = jnp.where(same(col_own[span, :], labels, j), wfull[ITERS - 1, span, :].astype(F32), 0.0).astype(BF16)
-            snd2 = dot(cfull[span, :], w, ((0,), (0,))).astype(BF16)
-            mids[side, :, j * LANES:(j + 1) * LANES] = snd2
-            enl[:, j * LANES:(j + 1) * LANES] = snd2
-        last = copy(enl, mid_got, m_s, m_r, site, partner)
-        last.start()
-        last.wait_recv()
-        mids[1 - side] = mid_got[...]
-        last.wait_send()
+            w = jnp.where(same(col_own[span, :], lab_in, j), wfull[ITERS - 1, span, :].astype(F32), 0.0).astype(BF16)
+            piece = dot(cfull[span, :], w, ((0,), (0,))).astype(BF16)
+            enl[:, j * LANES:(j + 1) * LANES] = piece
+            mid_copy(j).start()
+            mids[side, :, j * LANES:(j + 1) * LANES] = piece
+        for d in range(1, nblk):
+            src = (blk + nblk - d) % nblk
+            copy(newgot.at[src], newgot.at[src], n_s.at[d], n_r.at[src], site, partner).wait_recv()
+        for s in range(2):
+            total = jnp.zeros((rows, LANES), F32)
+            for q in range(nz):
+                total = total + newgot[2 * q + s].astype(F32)
+            fresh_out[s] = total
+        fresh_out[2] = col_own[own_rows(blk), :]
+        for j in range(blocks):
+            mid_copy(j).wait_recv()
+            mids[1 - side, :, j * LANES:(j + 1) * LANES] = mid_got[:, j * LANES:(j + 1) * LANES]
         swap.wait_send()
         label_copy().wait_send()
         cot_copy().wait_send()
+        for j in range(blocks):
+            mid_copy(j).wait_send()
         for c in w_copies() + corner_copies() + new_copies():
             c.wait_send()
         for at in range(ITERS):
@@ -254,9 +294,17 @@
                 c.wait_send()
 
 
-def grad_kernel(edge, mids, grad_left, grad_right):
+def grad_kernel(edge, mids, fresh, labels, grad_left, grad_right, new_left, new_right):
     grad_left[...] = dot(edge[...], mids[0], ((1,), (0,))).astype(BF16)
     grad_right[...] = dot(edge[...], mids[1], ((1,), (0,))).astype(BF16)
+
+    @pl.when(pl.program_id(0) == 0)
+    def _():
+        for s, out in enumerate((new_left, new_right)):
+            for j in range(labels.shape[1] // LANES):
+                at = slice(j * LANES, (j + 1) * LANES)
+                keep = fresh[2] == labels[:, at].astype(F32)
+                out[:, at] = jnp.where(keep, fresh[s], 0.0).astype(BF16)
 
 
 def body(nsite, nblk, corner, edge, proj_left, proj_right, charge, cot_left, cot_right):
@@ -265,35 +313,38 @@
     nz = nblk // 2
     pair = 2 * rows
     deep = rows * depth
-    chunk = deep // STEPS
+    chunk = width if deep % width == 0 else deep // 8
+    steps = deep // chunk
     edge_flat = edge[0].reshape(deep, width)
     left_flat = proj_left[0].reshape(deep, width)
     right_flat = proj_right[0].reshape(deep, width)
-    labels = jnp.broadcast_to(charge, (8, width))
 
     def whole(*shape):
         return pl.BlockSpec(shape, lambda k: (0,) * len(shape))
 
     def piece():
-        return pl.BlockSpec((chunk, width), lambda k: (k, 0))
+        return pl.BlockSpec((chunk, width), lambda k: (jnp.minimum(k, steps - 1), 0))
+
+    anywhere = pl.BlockSpec(memory_space=pl.ANY)
 
     aligned = rows % 16 == 0
     small = BF16 if aligned else F32
     dma = pltpu.SemaphoreType.DMA
-    mids, new_left, new_right = pl.pallas_call(
-        functools.partial(chain_kernel, nsite, nblk, STEPS),
-        grid=(STEPS,),
+    mids, fresh = pl.pallas_call(
+        functools.partial(chain_kernel, nsite, nblk, steps),
+        grid=(2 * steps,),
         out_shape=(
             jax.ShapeDtypeStruct((2, width, width), BF16),
-            jax.ShapeDtypeStruct((rows, width), BF16),
-            jax.ShapeDtypeStruct((rows, width), BF16),
+            jax.ShapeDtypeStruct((3, rows, LANES), F32),
         ),
         in_specs=[
-            whole(rows, width), piece(), piece(), piece(), whole(8, width),
+            whole(rows, width), piece(), anywhere, anywhere, whole(1, width),
             whole(rows, width), whole(rows, width),
         ],
-        out_specs=(whole(2, width, width), whole(rows, width), whole(rows, width)),
+        out_specs=(whole(2, width, width), whole(3, rows, LANES)),
         scratch_shapes=[
+            pltpu.VMEM((steps, width, chunk), BF16),
+            pltpu.VMEM((3, chunk, width), BF16),
             pltpu.VMEM((2, width, width), F32),
             pltpu.VMEM((width, width), BF16),
             pltpu.VMEM((width, width), BF16),
@@ -314,6 +365,7 @@
             pltpu.VMEM((width, LANES), small),
             pltpu.VMEM((nblk, rows, LANES), small),
             pltpu.VMEM((width, width), BF16),
+            dma((3,)),
             dma((2, nz)), dma((nblk,)),
             dma(()), dma(()),
             dma((nblk,)), dma((nblk,)),
@@ -322,23 +374,22 @@
             dma((ITERS, nz)), dma((ITERS, nz)),
             dma((ITERS, nz)), dma((ITERS, nz)),
             dma((nblk,)), dma((nblk,)),
-            dma(()), dma(()),
+            dma((width // LANES,)), dma((width // LANES,)),
         ],
         compiler_params=pltpu.CompilerParams(
-            collective_id=0, has_side_effects=True, vmem_limit_bytes=52 * 1024 * 1024,
+            collective_id=0, has_side_effects=True, vmem_limit_bytes=VMEM,
             dimension_semantics=("arbitrary",),
         ),
-    )(corner[0], edge_flat, left_flat, right_flat, labels, cot_left[0], cot_right[0])
-    grad_left, grad_right = pl.pallas_call(
+    )(corner[0], edge_flat, left_flat, right_flat, charge, cot_left[0], cot_right[0])
+    grad_left, grad_right, new_left, new_right = pl.pallas_call(
         grad_kernel,
-        grid=(STEPS,),
-        out_shape=(jax.ShapeDtypeStruct((deep, width), BF16),) * 2,
-        in_specs=[piece(), whole(2, width, width)],
-        out_specs=(piece(), piece()),
-        compiler_params=pltpu.CompilerParams(
-            vmem_limit_bytes=48 * 1024 * 1024, dimension_semantics=("arbitrary",)
-        ),
-    )(edge_flat, mids)
+        grid=(steps,),
+        out_shape=(jax.ShapeDtypeStruct((deep, width), BF16),) * 2
+        + (jax.ShapeDtypeStruct((rows, width), BF16),) * 2,
+        in_specs=[piece(), whole(2, width, width), whole(3, rows, LANES), whole(1, width)],
+        out_specs=(piece(), piece(), whole(rows, width), whole(rows, width)),
+        compiler_params=pltpu.CompilerParams(vmem_limit_bytes=VMEM, dimension_semantics=("arbitrary",)),
+    )(edge_flat, mids, fresh, charge)
     shape = (1, rows, depth, width)
     return (new_left[None], new_right[None], grad_left.reshape(shape), grad_right.reshape(shape))
 

time: 97.6 us -> 91.2 us (0.934)
  local copies, waits for them, and re-layouts: 5.81 us -> 0 us
    unnamed x10 -> x0, local copies, waits for them, and re-layouts: 5.81 us -> none
where the time goes in v2:
time: 91.2 us; the launch traced here: 90.7 us
  Pallas kernels  90 us (99%)
    pallas_call x1, Pallas kernels, body(): pl.pallas_call(functools.partial(chain_kernel, nsite, nblk, steps), grid=...  69.9 us
    pallas_call x1, Pallas kernels, body(): pl.pallas_call(grad_kernel, grid=(steps,), out_shape=(jax.ShapeDtypeStruc...  20.1 us

profile of v2, /device:TPU:0, one launch (start us, length us, event | category | flops | bytes accessed | tf_op | source)
XLA Modules:
  0.0 90.7 jit_solution(7896073390800769307)
XLA Ops:
  0.6 69.9 %shard_map.102 = (bf16[2,768,768]{2,1,0:T(8,128)(2,1)}, f32[3,96,128]{2,1,0:T(8,128)}) custom-call(bf16[96,768]{1,0:T(8,128)(2,1)} %bitcast.16, bf16[6144,768]{1,0:T(8,128)(2,1)} %bitcast.10, bf16[6144,768]{1,0:T(8,128)(2,1)} %bitcast.12, bf16[6144,768]{1,0:T(8,128)(2,1)} %bitcast.13, s32[1,768]{1,0:T(1,128)} %labels.3, f32[96,768]{1,0:T(8,128)} %bitcast.14, ...), custom_call_target="tpu_custom_call" | custom-call | tf_op jit(solution)/shard_map/pallas_call | solution.py:333
  70.6 20.1 %shard_map.103 = (bf16[6144,768]{1,0:T(8,128)(2,1)}, bf16[6144,768]{1,0:T(8,128)(2,1)}, bf16[96,768]{1,0:T(8,128)(2,1)}, bf16[96,768]{1,0:T(8,128)(2,1)}) custom-call(bf16[6144,768]{1,0:T(8,128)(2,1)} %bitcast.11, bf16[2,768,768]{2,1,0:T(8,128)(2,1)} %get-tuple-element.10.mids, f32[3,96,128]{2,1,0:T(8,128)} %get-tuple-element.11.fresh, s32[1,768]{1,0:T(1,128)} %labels.3), custom_call_target="tpu_custom_call" | custom-call | tf_op jit(solution)/shard_map/pallas_call | solution.py:384

commit v3 on v2

--- a/solution.py
+++ b/solution.py
@@ -22,9 +22,9 @@
     nsite, nblk, steps,
     corner, edge, left, right, labels, cot_left, cot_right,
     mids, fresh_out,
-    ebuf, pbuf, acc, snd, rcv, enl, cland, cfull, lab_in, lab_dst, col_own, col_dst, cotf, wsend, cpair,
+    ebuf, pbuf, acc, snd, rcv, enl, zland, cland, cfull, turned_corner, lab_in, lab_dst, col_own, col_dst, cotf, wsend, cpair,
     wzero, wfull, part, got, newp, newgot, mid_got,
-    f_s, c_s, c_r, l_s, l_r, w_s, w_r, p_s, p_r, e_s, e_r, r_s, r_r, a_s, a_r, n_s, n_r, m_s, m_r,
+    f_s, z_s, z_r, c_s, c_r, l_s, l_r, w_s, w_r, p_s, p_r, e_s, e_r, r_s, r_r, a_s, a_r, n_s, n_r, m_s, m_r,
 ):
     step = pl.program_id(0)
     rows, width = corner.shape
@@ -58,12 +58,29 @@
     def corner_slot(index):
         return cfull.at[own_rows(index)] if aligned else cland.at[index]
 
-    def corner_copies():
-        there = corner_slot(blk)
+    first = (site + side) % 2 == 1
+    near = site + 1 - 2 * (site % 2)
+    far = (site + nsite + 2 - 4 * ((site + jnp.where(first, 0, 1)) % 2)) % nsite
+
+    def plane_copies():
         out = []
-        for p in range(nz):
-            out.append(copy(corner, there, c_s.at[0, p], c_r.at[blk], up, 2 * p))
-            out.append(copy(corner, there, c_s.at[1, p], c_r.at[blk], down, 2 * p + 1))
+        for d in range(1, nz):
+            to = 2 * ((z + d) % nz) + side
+            out.append(copy(corner, zland.at[z], z_s.at[d], z_r.at[z], site, to))
+        return out
+
+    def near_copy(d):
+        at = (z + d) % nz
+        src = corner if d == 0 else zland.at[at]
+        slot = 2 * at + side
+        return copy(src, corner_slot(slot), c_s.at[0, d], c_r.at[slot], near, 2 * z + site % 2)
+
+    def far_copies(d):
+        out = []
+        for c in range(2):
+            slot = 2 * ((z + d) % nz) + c
+            here = corner_slot(slot)
+            out.append(copy(here, here, c_s.at[1 + c, d], c_r.at[slot], far, partner))
         return out
 
     def w_copies():
@@ -109,6 +126,7 @@
                 pl.semaphore_signal(barrier, inc=1, device_id={"site": where, "blk": b}, device_id_type=pl.DeviceIdType.MESH)
         for d in range(1, nblk):
             pl.semaphore_signal(barrier, inc=1, device_id={"site": site, "blk": (blk + d) % nblk}, device_id_type=pl.DeviceIdType.MESH)
+        pl.semaphore_signal(barrier, inc=1, device_id={"site": far, "blk": partner}, device_id_type=pl.DeviceIdType.MESH)
         lab_in[...] = jnp.broadcast_to(labels[...], lab_in.shape)
         columns(lab_in, col_own)
         mine = col_own[own_rows(blk), :]
@@ -124,11 +142,39 @@
 
     @pl.when(step == 1)
     def _():
-        pl.semaphore_wait(pltpu.get_barrier_semaphore(), 3 * nblk - 1)
+        pl.semaphore_wait(pltpu.get_barrier_semaphore(), 3 * nblk)
         label_copy().start()
         cot_copy().start()
-        for c in w_copies() + corner_copies():
+        for c in w_copies() + plane_copies() + [near_copy(0)]:
             c.start()
+
+    def relay_near(d):
+        @pl.when(step == relay_step(d))
+        def _():
+            at = (z + d) % nz
+            copy(zland.at[at], zland.at[at], z_s.at[d], z_r.at[at], site, partner).wait_recv()
+            near_copy(d).start()
+
+    def relay_far(d):
+        @pl.when(jnp.logical_and(step == min(relay_step(d) + 3, 2 * steps - 1), first))
+        def _():
+            for c in range(2):
+                slot = 2 * ((z + d) % nz) + c
+                corner_wait(slot)
+            for c in far_copies(d):
+                c.start()
+
+    def relay_step(d):
+        return 2 + d * (2 * steps - 4) // nz
+
+    def corner_wait(slot):
+        there = corner_slot(slot)
+        copy(there, there, c_s.at[0, 0], c_r.at[slot], site, partner).wait_recv()
+
+    for d in range(1, nz):
+        relay_near(d)
+    for d in range(nz):
+        relay_far(d)
 
     @pl.when(step + 2 < 2 * steps)
     def _():
@@ -211,10 +257,11 @@
             out.append(copy(newp.at[own_rows(to)], newgot.at[blk], n_s.at[d], n_r.at[blk], site, to))
         return out
 
-    def corner_wait():
-        for q in range(nblk):
-            there = corner_slot(q)
-            copy(there, there, c_s.at[0, 0], c_r.at[q], site, partner).wait_recv()
+    def corner_ready():
+        @pl.when(jnp.logical_not(first))
+        def _():
+            for q in range(nblk):
+                corner_wait(q)
         if not aligned:
             for q in range(nz):
                 both = [cland[2 * q].astype(F32), cland[2 * q + 1].astype(F32)]
@@ -232,9 +279,11 @@
                 total = total + jnp.where(same(mine, lab_in, j), piece, 0.0)
             newp[rows_i, :] = total.astype(newp.dtype)
 
-    def mid_copy(j):
-        here = slice(j * LANES, (j + 1) * LANES)
-        return copy(enl.at[:, here], mid_got.at[:, here], m_s.at[j], m_r.at[j], site, partner)
+    groups = [range(j, min(blocks, j + 2)) for j in range(0, blocks, 2)]
+
+    def mid_copy(g):
+        here = slice(g[0] * LANES, (g[-1] + 1) * LANES)
+        return copy(enl.at[:, here], mid_got.at[:, here], m_s.at[g[0]], m_r.at[g[0]], site, partner)
 
     @pl.when(step == 2 * steps - 1)
     def _():
@@ -255,21 +304,25 @@
             for c in reduce_copies(at):
                 c.start()
             if at == ITERS - 1:
-                corner_wait()
+                corner_ready()
+                turned_corner[...] = cfull[...].T
                 new_partial()
                 for c in new_copies():
                     c.start()
                 newgot[blk] = newp[own_rows(blk), :]
             reduce_and_send(at)
         gather_wait(ITERS - 1)
-        for j in range(blocks):
-            lo, hi = window(j)
+        for g in groups:
+            lo, hi = max(0, g[0] - 1), min(blocks, g[-1] + 2)
             span = slice(lo * LANES, hi * LANES)
-            w = jnp.where(same(col_own[span, :], lab_in, j), wfull[ITERS - 1, span, :].astype(F32), 0.0).astype(BF16)
-            piece = dot(cfull[span, :], w, ((0,), (0,))).astype(BF16)
-            enl[:, j * LANES:(j + 1) * LANES] = piece
-            mid_copy(j).start()
-            mids[side, :, j * LANES:(j + 1) * LANES] = piece
+            here = slice(g[0] * LANES, (g[-1] + 1) * LANES)
+            last = wfull[ITERS - 1, span, :].astype(F32)
+            mine = col_own[span, :]
+            w = jnp.concatenate([jnp.where(same(mine, lab_in, j), last, 0.0) for j in g], axis=1).astype(BF16)
+            piece = dot(turned_corner[:, span], w, ((1,), (0,))).astype(BF16)
+            enl[:, here] = piece
+            mid_copy(g).start()
+            mids[side, :, here] = piece
         for d in range(1, nblk):
             src = (blk + nblk - d) % nblk
             copy(newgot.at[src], newgot.at[src], n_s.at[d], n_r.at[src], site, partner).wait_recv()
@@ -279,16 +332,25 @@
                 total = total + newgot[2 * q + s].astype(F32)
             fresh_out[s] = total
         fresh_out[2] = col_own[own_rows(blk), :]
-        for j in range(blocks):
-            mid_copy(j).wait_recv()
-            mids[1 - side, :, j * LANES:(j + 1) * LANES] = mid_got[:, j * LANES:(j + 1) * LANES]
+        for g in groups:
+            here = slice(g[0] * LANES, (g[-1] + 1) * LANES)
+            mid_copy(g).wait_recv()
+            mids[1 - side, :, here] = mid_got[:, here]
         swap.wait_send()
         label_copy().wait_send()
         cot_copy().wait_send()
-        for j in range(blocks):
-            mid_copy(j).wait_send()
-        for c in w_copies() + corner_copies() + new_copies():
+        for g in groups:
+            mid_copy(g).wait_send()
+        for c in w_copies() + plane_copies() + new_copies():
             c.wait_send()
+        for d in range(nz):
+            near_copy(d).wait_send()
+
+        @pl.when(first)
+        def _():
+            for d in range(nz):
+                for c in far_copies(d):
+                    c.wait_send()
         for at in range(ITERS):
             for c in reduce_copies(at) + gather_copies(at):
                 c.wait_send()
@@ -349,7 +411,9 @@
             pltpu.VMEM((width, width), BF16),
             pltpu.VMEM((width, width), BF16),
             pltpu.VMEM((width, width), BF16),
+            pltpu.VMEM((nz, rows, width), BF16),
             pltpu.VMEM((1, 16, LANES) if aligned else (nblk, rows, width), BF16),
+            pltpu.VMEM((width, width), BF16),
             pltpu.VMEM((width, width), BF16),
             pltpu.VMEM((8, width), jnp.int32),
             pltpu.VMEM((8, width), jnp.int32),
@@ -366,7 +430,8 @@
             pltpu.VMEM((nblk, rows, LANES), small),
             pltpu.VMEM((width, width), BF16),
             dma((3,)),
-            dma((2, nz)), dma((nblk,)),
+            dma((nz,)), dma((nz,)),
+            dma((3, nz)), dma((nblk,)),
             dma(()), dma(()),
             dma((nblk,)), dma((nblk,)),
             dma(()), dma(()),

time: 91.2 us -> 93.9 us (1.030)
  Pallas kernels: 90 us -> 92.8 us
    pallas_call x1, Pallas kernels: 69.9 us -> 72.6 us  [body(): pl.pallas_call(functools.partial(chain_kernel, nsite, nblk, steps), grid=...]
where the time goes in v3:
time: 93.9 us; the launch traced here: 93.4 us
  Pallas kernels  92.8 us (99%)
    pallas_call x1, Pallas kernels, body(): pl.pallas_call(functools.partial(chain_kernel, nsite, nblk, steps), grid=...  72.6 us
    pallas_call x1, Pallas kernels, body(): pl.pallas_call(grad_kernel, grid=(steps,), out_shape=(jax.ShapeDtypeStruc...  20.1 us

profile of v3, /device:TPU:0, one launch (start us, length us, event | category | flops | bytes accessed | tf_op | source)
XLA Modules:
  0.0 93.4 jit_solution(17617667424897486338)
XLA Ops:
  0.6 72.6 %shard_map.102 = (bf16[2,768,768]{2,1,0:T(8,128)(2,1)}, f32[3,96,128]{2,1,0:T(8,128)}) custom-call(bf16[96,768]{1,0:T(8,128)(2,1)} %bitcast.16, bf16[6144,768]{1,0:T(8,128)(2,1)} %bitcast.10, bf16[6144,768]{1,0:T(8,128)(2,1)} %bitcast.12, bf16[6144,768]{1,0:T(8,128)(2,1)} %bitcast.13, s32[1,768]{1,0:T(1,128)} %labels.3, f32[96,768]{1,0:T(8,128)} %bitcast.14, ...), custom_call_target="tpu_custom_call" | custom-call | tf_op jit(solution)/shard_map/pallas_call | solution.py:395
  73.3 20.1 %shard_map.103 = (bf16[6144,768]{1,0:T(8,128)(2,1)}, bf16[6144,768]{1,0:T(8,128)(2,1)}, bf16[96,768]{1,0:T(8,128)(2,1)}, bf16[96,768]{1,0:T(8,128)(2,1)}) custom-call(bf16[6144,768]{1,0:T(8,128)(2,1)} %bitcast.11, bf16[2,768,768]{2,1,0:T(8,128)(2,1)} %get-tuple-element.10.mids, f32[3,96,128]{2,1,0:T(8,128)} %get-tuple-element.11.fresh, s32[1,768]{1,0:T(1,128)} %labels.3), custom_call_target="tpu_custom_call" | custom-call | tf_op jit(solution)/shard_map/pallas_call | solution.py:449

commit v4 on v2

--- a/solution.py
+++ b/solution.py
@@ -21,10 +21,10 @@
 def chain_kernel(
     nsite, nblk, steps,
     corner, edge, left, right, labels, cot_left, cot_right,
-    mids, fresh_out,
-    ebuf, pbuf, acc, snd, rcv, enl, cland, cfull, lab_in, lab_dst, col_own, col_dst, cotf, wsend, cpair,
-    wzero, wfull, part, got, newp, newgot, mid_got,
-    f_s, c_s, c_r, l_s, l_r, w_s, w_r, p_s, p_r, e_s, e_r, r_s, r_r, a_s, a_r, n_s, n_r, m_s, m_r,
+    turned_out, w_out, col_out, fresh_out,
+    ebuf, estore, tbuf, cother, wother, pbuf, acc, snd, rcv, enl, cland, cfull, lab_in, lab_dst, col_own, col_dst, cotf, wsend, cpair,
+    wzero, wfull, part, got, newp, newgot,
+    f_s, c_s, c_r, l_s, l_r, w_s, w_r, p_s, p_r, e_s, e_r, r_s, r_r, a_s, a_r, n_s, n_r, o_s, o_r, v_s, v_r, t_s,
 ):
     step = pl.program_id(0)
     rows, width = corner.shape
@@ -140,6 +140,7 @@
     def _():
         turned = edge[...].T
         ebuf[step] = turned
+        estore[step] = edge[...]
         acc[0] += dot(turned, pbuf[step % 3], ((1,), (0,)))
 
     @pl.when(step == steps)
@@ -232,9 +233,22 @@
                 total = total + jnp.where(same(mine, lab_in, j), piece, 0.0)
             newp[rows_i, :] = total.astype(newp.dtype)
 
-    def mid_copy(j):
-        here = slice(j * LANES, (j + 1) * LANES)
-        return copy(enl.at[:, here], mid_got.at[:, here], m_s.at[j], m_r.at[j], site, partner)
+    halves = (range(0, steps // 2), range(steps // 2, steps))
+
+    def store_copy(which, k, slot):
+        return pltpu.make_async_copy(
+            tbuf.at[slot], turned_out.at[which, pl.ds(k * chunk, chunk)], t_s.at[slot]
+        )
+
+    def edge_corner(which, full, chunks, before):
+        for slot, k in enumerate(chunks):
+            if before is not None and slot < len(before[1]):
+                store_copy(before[0], before[1][slot], slot).wait()
+            tbuf[slot] = dot(estore[k], full[...], ((1,), (1,))).astype(BF16)
+            store_copy(which, k, slot).start()
+        if before is not None:
+            for slot in range(len(chunks), len(before[1])):
+                store_copy(before[0], before[1][slot], slot).wait()
 
     @pl.when(step == 2 * steps - 1)
     def _():
@@ -248,28 +262,39 @@
         swap = copy(snd, rcv, e_s, e_r, site, partner)
         swap.wait_recv()
         enl[...] = (acc[1] + rcv[...].astype(F32)).astype(BF16)
+        forward = copy(cfull, cother, o_s, o_r, site, partner)
+        w_swap = copy(wfull.at[ITERS - 1], wother, v_s, v_r, site, partner)
+        before = None
         for at in range(ITERS):
             if at:
                 gather_wait(at - 1)
             back_partial(at)
             for c in reduce_copies(at):
                 c.start()
+            if at == 0:
+                corner_wait()
+                forward.start()
+                edge_corner(side, cfull, halves[0], before)
+                before = (side, halves[0])
             if at == ITERS - 1:
-                corner_wait()
+                forward.wait_recv()
                 new_partial()
                 for c in new_copies():
                     c.start()
                 newgot[blk] = newp[own_rows(blk), :]
+                edge_corner(1 - side, cother, halves[0], before)
+                before = (1 - side, halves[0])
             reduce_and_send(at)
+            if at == 0:
+                edge_corner(side, cfull, halves[1], before)
+                before = (side, halves[1])
+            if at == ITERS - 1:
+                edge_corner(1 - side, cother, halves[1], before)
+                before = (1 - side, halves[1])
         gather_wait(ITERS - 1)
-        for j in range(blocks):
-            lo, hi = window(j)
-            span = slice(lo * LANES, hi * LANES)
-            w = jnp.where(same(col_own[span, :], lab_in, j), wfull[ITERS - 1, span, :].astype(F32), 0.0).astype(BF16)
-            piece = dot(cfull[span, :], w, ((0,), (0,))).astype(BF16)
-            enl[:, j * LANES:(j + 1) * LANES] = piece
-            mid_copy(j).start()
-            mids[side, :, j * LANES:(j + 1) * LANES] = piece
+        w_swap.start()
+        w_out[side] = wfull[ITERS - 1]
+        col_out[...] = col_own[...]
         for d in range(1, nblk):
             src = (blk + nblk - d) % nblk
             copy(newgot.at[src], newgot.at[src], n_s.at[d], n_r.at[src], site, partner).wait_recv()
@@ -279,14 +304,15 @@
                 total = total + newgot[2 * q + s].astype(F32)
             fresh_out[s] = total
         fresh_out[2] = col_own[own_rows(blk), :]
-        for j in range(blocks):
-            mid_copy(j).wait_recv()
-            mids[1 - side, :, j * LANES:(j + 1) * LANES] = mid_got[:, j * LANES:(j + 1) * LANES]
+        w_swap.wait_recv()
+        w_out[1 - side] = wother[...]
+        for slot, k in enumerate(before[1]):
+            store_copy(before[0], k, slot).wait()
+        w_swap.wait_send()
+        forward.wait_send()
         swap.wait_send()
         label_copy().wait_send()
         cot_copy().wait_send()
-        for j in range(blocks):
-            mid_copy(j).wait_send()
         for c in w_copies() + corner_copies() + new_copies():
             c.wait_send()
         for at in range(ITERS):
@@ -294,9 +320,26 @@
                 c.wait_send()
 
 
-def grad_kernel(edge, mids, fresh, labels, grad_left, grad_right, new_left, new_right):
-    grad_left[...] = dot(edge[...], mids[0], ((1,), (0,))).astype(BF16)
-    grad_right[...] = dot(edge[...], mids[1], ((1,), (0,))).astype(BF16)
+def grad_kernel(turned, folded, column, fresh, labels, grad_left, grad_right, new_left, new_right, wide):
+    blocks = labels.shape[1] // LANES
+    groups = []
+    for j in range(0, blocks, 2):
+        top = min(blocks, j + 2)
+        groups.append((slice(max(0, j - 1) * LANES, min(blocks, top + 1) * LANES), range(j, top)))
+
+    @pl.when(pl.program_id(0) == 0)
+    def _():
+        for s in range(2):
+            for span, inside in groups:
+                for j in inside:
+                    at = slice(j * LANES, (j + 1) * LANES)
+                    keep = column[span, :] == labels[:, at].astype(F32)
+                    wide[s, span, at] = jnp.where(keep, folded[s, span, :].astype(F32), 0.0).astype(BF16)
+
+    for s, out in enumerate((grad_left, grad_right)):
+        for span, inside in groups:
+            here = slice(inside[0] * LANES, (inside[-1] + 1) * LANES)
+            out[:, here] = dot(turned[s, :, span], wide[s, span, here], ((1,), (0,))).astype(BF16)
 
     @pl.when(pl.program_id(0) == 0)
     def _():
@@ -330,20 +373,26 @@
     aligned = rows % 16 == 0
     small = BF16 if aligned else F32
     dma = pltpu.SemaphoreType.DMA
-    mids, fresh = pl.pallas_call(
+    turned, folded, column, fresh = pl.pallas_call(
         functools.partial(chain_kernel, nsite, nblk, steps),
         grid=(2 * steps,),
         out_shape=(
-            jax.ShapeDtypeStruct((2, width, width), BF16),
+            jax.ShapeDtypeStruct((2, deep, width), BF16),
+            jax.ShapeDtypeStruct((2, width, LANES), BF16),
+            jax.ShapeDtypeStruct((width, LANES), F32),
             jax.ShapeDtypeStruct((3, rows, LANES), F32),
         ),
         in_specs=[
             whole(rows, width), piece(), anywhere, anywhere, whole(1, width),
             whole(rows, width), whole(rows, width),
         ],
-        out_specs=(whole(2, width, width), whole(3, rows, LANES)),
+        out_specs=(anywhere, whole(2, width, LANES), whole(width, LANES), whole(3, rows, LANES)),
         scratch_shapes=[
             pltpu.VMEM((steps, width, chunk), BF16),
+            pltpu.VMEM((steps, chunk, width), BF16),
+            pltpu.VMEM((steps - steps // 2, chunk, width), BF16),
+            pltpu.VMEM((width, width), BF16),
+            pltpu.VMEM((width, LANES), BF16),
             pltpu.VMEM((3, chunk, width), BF16),
             pltpu.VMEM((2, width, width), F32),
             pltpu.VMEM((width, width), BF16),
@@ -364,7 +413,6 @@
             pltpu.VMEM((ITERS, nz, pair, LANES), BF16),
             pltpu.VMEM((width, LANES), small),
             pltpu.VMEM((nblk, rows, LANES), small),
-            pltpu.VMEM((width, width), BF16),
             dma((3,)),
             dma((2, nz)), dma((nblk,)),
             dma(()), dma(()),
@@ -374,7 +422,9 @@
             dma((ITERS, nz)), dma((ITERS, nz)),
             dma((ITERS, nz)), dma((ITERS, nz)),
             dma((nblk,)), dma((nblk,)),
-            dma((width // LANES,)), dma((width // LANES,)),
+            dma(()), dma(()),
+            dma(()), dma(()),
+            dma((steps - steps // 2,)),
         ],
         compiler_params=pltpu.CompilerParams(
             collective_id=0, has_side_effects=True, vmem_limit_bytes=VMEM,
@@ -386,10 +436,14 @@
         grid=(steps,),
         out_shape=(jax.ShapeDtypeStruct((deep, width), BF16),) * 2
         + (jax.ShapeDtypeStruct((rows, width), BF16),) * 2,
-        in_specs=[piece(), whole(2, width, width), whole(3, rows, LANES), whole(1, width)],
+        in_specs=[
+            pl.BlockSpec((2, chunk, width), lambda k: (0, k, 0)), whole(2, width, LANES),
+            whole(width, LANES), whole(3, rows, LANES), whole(1, width),
+        ],
         out_specs=(piece(), piece(), whole(rows, width), whole(rows, width)),
+        scratch_shapes=[pltpu.VMEM((2, width, width), BF16)],
         compiler_params=pltpu.CompilerParams(vmem_limit_bytes=VMEM, dimension_semantics=("arbitrary",)),
-    )(edge_flat, mids, fresh, charge)
+    )(turned, folded, column, fresh, charge)
     shape = (1, rows, depth, width)
     return (new_left[None], new_right[None], grad_left.reshape(shape), grad_right.reshape(shape))
 

time: 91.2 us -> 87.6 us (0.961)
  Pallas kernels: 90 us -> 86.6 us
    pallas_call x1, Pallas kernels: 69.9 us -> 67.3 us  [body(): pl.pallas_call(functools.partial(chain_kernel, nsite, nblk, steps), grid=...]
where the time goes in v4:
time: 87.6 us; the launch traced here: 87.3 us
  Pallas kernels  86.6 us (99%)
    pallas_call x1, Pallas kernels, body(): pl.pallas_call(functools.partial(chain_kernel, nsite, nblk, steps), grid=...  67.3 us
    pallas_call x1, Pallas kernels, body(): pl.pallas_call(grad_kernel, grid=(steps,), out_shape=(jax.ShapeDtypeStruc...  19.3 us

profile of v4, /device:TPU:0, one launch (start us, length us, event | category | flops | bytes accessed | tf_op | source)
XLA Modules:
  0.0 87.3 jit_solution(16015754878090200236)
XLA Ops:
  0.6 67.3 %shard_map.102 = (bf16[2,6144,768]{2,1,0:T(8,128)(2,1)}, bf16[2,768,128]{2,1,0:T(8,128)(2,1)}, f32[768,128]{1,0:T(8,128)}, f32[3,96,128]{2,1,0:T(8,128)}) custom-call(bf16[96,768]{1,0:T(8,128)(2,1)} %bitcast.15, bf16[6144,768]{1,0:T(8,128)(2,1)} %bitcast.10, bf16[6144,768]{1,0:T(8,128)(2,1)} %bitcast.11, bf16[6144,768]{1,0:T(8,128)(2,1)} %bitcast.12, ...), custom_call_target="tpu_custom_call" | custom-call | tf_op jit(solution)/shard_map/pallas_call | solution.py:376
  68.0 19.3 %shard_map.103 = (bf16[6144,768]{1,0:T(8,128)(2,1)}, bf16[6144,768]{1,0:T(8,128)(2,1)}, bf16[96,768]{1,0:T(8,128)(2,1)}, bf16[96,768]{1,0:T(8,128)(2,1)}) custom-call(bf16[2,6144,768]{2,1,0:T(8,128)(2,1)} %get-tuple-element.12.turned, bf16[2,768,128]{2,1,0:T(8,128)(2,1)} %get-tuple-element.13.folded, f32[768,128]{1,0:T(8,128)} %get-tuple-element.14.column, ...), custom_call_target="tpu_custom_call" | custom-call | tf_op jit(solution)/shard_map/pallas_call | solution.py:434

commit v5 on v4

--- a/solution.py
+++ b/solution.py
@@ -320,7 +320,7 @@
                 c.wait_send()
 
 
-def grad_kernel(turned, folded, column, fresh, labels, grad_left, grad_right, new_left, new_right, wide):
+def grad_kernel(turned_left, turned_right, folded, column, fresh, labels, grad_left, grad_right, new_left, new_right, wide):
     blocks = labels.shape[1] // LANES
     groups = []
     for j in range(0, blocks, 2):
@@ -336,10 +336,10 @@
                     keep = column[span, :] == labels[:, at].astype(F32)
                     wide[s, span, at] = jnp.where(keep, folded[s, span, :].astype(F32), 0.0).astype(BF16)
 
-    for s, out in enumerate((grad_left, grad_right)):
+    for s, (turned, out) in enumerate(((turned_left, grad_left), (turned_right, grad_right))):
         for span, inside in groups:
             here = slice(inside[0] * LANES, (inside[-1] + 1) * LANES)
-            out[:, here] = dot(turned[s, :, span], wide[s, span, here], ((1,), (0,))).astype(BF16)
+            out[:, here] = dot(turned[0, :, span], wide[s, span, here], ((1,), (0,))).astype(BF16)
 
     @pl.when(pl.program_id(0) == 0)
     def _():
@@ -431,19 +431,22 @@
             dimension_semantics=("arbitrary",),
         ),
     )(corner[0], edge_flat, left_flat, right_flat, charge, cot_left[0], cot_right[0])
+    slab = 512 if deep % 512 == 0 else chunk
+    out_piece = pl.BlockSpec((slab, width), lambda k: (k, 0))
     grad_left, grad_right, new_left, new_right = pl.pallas_call(
         grad_kernel,
-        grid=(steps,),
+        grid=(deep // slab,),
         out_shape=(jax.ShapeDtypeStruct((deep, width), BF16),) * 2
         + (jax.ShapeDtypeStruct((rows, width), BF16),) * 2,
         in_specs=[
-            pl.BlockSpec((2, chunk, width), lambda k: (0, k, 0)), whole(2, width, LANES),
+            pl.BlockSpec((1, slab, width), lambda k: (0, k, 0)),
+            pl.BlockSpec((1, slab, width), lambda k: (1, k, 0)), whole(2, width, LANES),
             whole(width, LANES), whole(3, rows, LANES), whole(1, width),
         ],
-        out_specs=(piece(), piece(), whole(rows, width), whole(rows, width)),
+        out_specs=(out_piece, out_piece, whole(rows, width), whole(rows, width)),
         scratch_shapes=[pltpu.VMEM((2, width, width), BF16)],
         compiler_params=pltpu.CompilerParams(vmem_limit_bytes=VMEM, dimension_semantics=("arbitrary",)),
-    )(turned, folded, column, fresh, charge)
+    )(turned, turned, folded, column, fresh, charge)
     shape = (1, rows, depth, width)
     return (new_left[None], new_right[None], grad_left.reshape(shape), grad_right.reshape(shape))
 

time: 87.6 us -> 89.1 us (1.017)
  Pallas kernels: 86.6 us -> 87.9 us
    pallas_call x1, Pallas kernels: 19.3 us -> 20.6 us  [body(): pl.pallas_call(grad_kernel, grid=(deep // slab,), out_shape=(jax.ShapeDty...]
where the time goes in v5:
time: 89.1 us; the launch traced here: 88.6 us
  Pallas kernels  87.9 us (99%)
    pallas_call x1, Pallas kernels, body(): pl.pallas_call(functools.partial(chain_kernel, nsite, nblk, steps), grid=...  67.3 us
    pallas_call x1, Pallas kernels, body(): pl.pallas_call(grad_kernel, grid=(deep // slab,), out_shape=(jax.ShapeDty...  20.6 us

profile of v5, /device:TPU:0, one launch (start us, length us, event | category | flops | bytes accessed | tf_op | source)
XLA Modules:
  0.0 88.6 jit_solution(14378511373079726932)
XLA Ops:
  0.6 67.3 %shard_map.102 = (bf16[2,6144,768]{2,1,0:T(8,128)(2,1)}, bf16[2,768,128]{2,1,0:T(8,128)(2,1)}, f32[768,128]{1,0:T(8,128)}, f32[3,96,128]{2,1,0:T(8,128)}) custom-call(bf16[96,768]{1,0:T(8,128)(2,1)} %bitcast.15, bf16[6144,768]{1,0:T(8,128)(2,1)} %bitcast.10, bf16[6144,768]{1,0:T(8,128)(2,1)} %bitcast.11, bf16[6144,768]{1,0:T(8,128)(2,1)} %bitcast.12, ...), custom_call_target="tpu_custom_call" | custom-call | tf_op jit(solution)/shard_map/pallas_call | solution.py:376
  68.0 20.6 %shard_map.103 = (bf16[6144,768]{1,0:T(8,128)(2,1)}, bf16[6144,768]{1,0:T(8,128)(2,1)}, bf16[96,768]{1,0:T(8,128)(2,1)}, bf16[96,768]{1,0:T(8,128)(2,1)}) custom-call(bf16[2,6144,768]{2,1,0:T(8,128)(2,1)} %get-tuple-element.12.turned_left.turned_right, bf16[2,6144,768]{2,1,0:T(8,128)(2,1)} %get-tuple-element.12.turned_left.turned_right, ...), custom_call_target="tpu_custom_call" | custom-call | tf_op jit(solution)/shard_map/pallas_call | solution.py:436
